TPU v7x, 32 devices: a whole 2x2x4 slice. The times are simulated.
32 devices in a mesh: row: 4 (over y, core), col: 8 (over z, x).
Axes of the slice: x: 2, y: 2, z: 4, core: 2. Of those that a mesh axis runs over, the one named last changes fastest.
Arguments:
- alignment: bfloat16 [64, 384, 256], P('row', 'col'), may hold values from -6.5 to 6.5
- pair_features: float32 [384, 384, 128], P('row', 'col'), may hold values from -6 to 6
- query_weight: bfloat16 [256, 256], replicated, may hold values from -25 to 25
- key_weight: bfloat16 [256, 256], replicated, may hold values from -0.375 to 0.375
- value_projection: bfloat16 [256, 256], replicated, may hold values from -0.375 to 0.375
- gate_projection: bfloat16 [256, 256], replicated, may hold values from -0.375 to 0.375
- gate_bias: float32 [256], replicated, may hold values from -4 to 4
- output_projection: bfloat16 [256, 256], replicated, may hold values from -0.375 to 0.375
- left_projection: bfloat16 [256, 32], replicated, may hold values from -0.375 to 0.375
- right_projection: bfloat16 [256, 32], replicated, may hold values from -0.375 to 0.375
- outer_weight: bfloat16 [1024, 128], replicated, may hold values from -0.75 to 0.75
- outer_bias: float32 [128], replicated, may hold values from -3 to 3
- expand_weight: bfloat16 [128, 512], replicated, may hold values from -0.5 to 0.5
- shrink_weight: bfloat16 [512, 128], replicated, may hold values from -0.25 to 0.25
- cotangent: float32 [384, 384, 128], P('row', 'col'), may hold values from -6 to 6
Outputs:
- updated: bfloat16 [64, 384, 256], P('row', 'col')
- pair_out: float32 [384, 384, 128], P('row', 'col')
- grad_left: float32 [64, 12288], P('col', 'row')
- grad_right: float32 [64, 12288], P('row', 'col')
All inputs are finite; a program needn't handle non-finite values.
Results may differ from a plain program's by a relative error of at most 0.017.
Values may be sent and summed in bfloat16 or wider, within the bound.
No kernel may reach another device: no remote copies, remote signals or barrier semaphores. Data moves between devices by JAX's collectives and lax.ppermute only.
A program may use at most 192 MiB of HBM per device.

v0:
```python
import functools

import jax
import jax.numpy as jnp
from jax import lax
from jax.experimental import pallas as pl
from jax.experimental.pallas import tpu as pltpu
from jax.sharding import PartitionSpec as P

ATTENTION_HEADS = 8
HEAD_WIDTH = 32
FACTOR_WIDTH = 32
PAIR_W = 128
EPSILON = 1e-05

LANES = 128
MXU_SIDE = 256
HALF = 64
TILE = 32
CHUNK = 4
UNIT = 4


def dot_nn(a, b):
    return lax.dot_general(a, b, (((1,), (0,)), ((), ())), preferred_element_type=jnp.float32)


def dot_nt(a, b):
    return lax.dot_general(a, b, (((1,), (1,)), ((), ())), preferred_element_type=jnp.float32)


def layer_normalise(rows):
    rows = rows.astype(jnp.float32)
    average = jnp.mean(rows, axis=-1, keepdims=True)
    centred = rows - average
    variance = jnp.mean(centred * centred, axis=-1, keepdims=True)
    return centred * lax.rsqrt(variance + EPSILON)


def attend_kernel(
    place_ref, x_ref, wq_ref, wk_ref, wv_ref, wg_ref, bias_ref, wo_ref, wl_ref, wr_ref, *refs,
):
    *upd_refs, factor_ref, q_s, k_s, v_s, g_s, a_s, w_s, bias_s, project_s, upd_s, ordered_s, sems = refs
    parts, residues, part_seqs, width = x_ref.shape
    seqs = parts * part_seqs
    sources = (wq_ref, wk_ref, wv_ref, wg_ref, wo_ref, bias_ref, wl_ref, wr_ref)
    targets = [w_s.at[n] for n in range(5)] + [bias_s, project_s.at[0], project_s.at[1]]
    copies = [pltpu.make_async_copy(a, b, sems.at[n]) for n, (a, b) in enumerate(zip(sources, targets))]
    for copy in copies:
        copy.start()
    x = jnp.concatenate([x_ref[s, r] for r in range(residues) for s in range(parts)], axis=0)
    normed = layer_normalise(x).astype(jnp.bfloat16)
    for n, ref in enumerate((q_s, k_s, v_s)):
        copies[n].wait()
        ref[...] = dot_nn(normed, w_s[n]).astype(jnp.bfloat16)
    copies[3].wait()
    copies[5].wait()
    g_s[...] = jax.nn.sigmoid(dot_nn(normed, w_s[3]) + bias_s[...])

    head_of = lax.broadcasted_iota(jnp.int32, (1, width), 1) // HEAD_WIDTH
    masks = [(head_of == h).astype(jnp.float32) for h in range(ATTENTION_HEADS)]
    masks_low = [m.astype(jnp.bfloat16) for m in masks]

    def one_residue(r, carry):
        rows = pl.ds(pl.multiple_of(r * seqs, seqs), seqs)
        query = q_s[rows, :]
        spread_query = jnp.concatenate([query * m for m in masks_low], axis=0)
        scores = dot_nt(spread_query, k_s[rows, :]) * HEAD_WIDTH ** (-0.5)
        raised = jnp.exp(scores - jnp.max(scores, axis=-1, keepdims=True))
        inverse = 1.0 / jnp.sum(raised, axis=-1, keepdims=True)
        blended = dot_nn(raised.astype(jnp.bfloat16), v_s[rows, :]) * inverse
        total = blended[:seqs] * masks[0]
        for h in range(1, ATTENTION_HEADS):
            total = total + blended[h * seqs:(h + 1) * seqs] * masks[h]
        a_s[rows, :] = (g_s[rows, :] * total).astype(jnp.bfloat16)
        return carry

    lax.fori_loop(0, residues, one_residue, 0, unroll=6 if residues % 6 == 0 else 2)

    copies[4].wait()
    updated = (x.astype(jnp.float32) + dot_nn(a_s[...], w_s[4])).astype(jnp.bfloat16)
    for r in range(residues):
        for s in range(parts):
            begin = r * seqs + s * part_seqs
            upd_s[s, :, r * width:(r + 1) * width] = updated[begin:begin + part_seqs]
    leaving = []
    for k, ref in enumerate(upd_refs):
        ordered_s[k] = upd_s[place_ref[0] ^ k]
        leaving.append(pltpu.make_async_copy(ordered_s.at[k], ref, sems.at[len(sources) + k]))
        leaving[k].start()
    factor_norm = layer_normalise(updated).astype(jnp.bfloat16)
    copies[6].wait()
    copies[7].wait()
    project = project_s[...].reshape(2 * FACTOR_WIDTH, width)
    for p in range(residues // 2):
        both = dot_nt(project, factor_norm[p * 2 * seqs:(p + 1) * 2 * seqs]).astype(jnp.bfloat16)
        for n in range(parts):
            factor_ref[n, 0, p] = both[:FACTOR_WIDTH]
            factor_ref[n, 1, p] = both[FACTOR_WIDTH:]
    for copy in leaving:
        copy.wait()


def whole_block(shape):
    return pl.BlockSpec(shape, lambda *_: (0,) * len(shape))


def in_hbm(*arrays):
    return [pltpu.with_memory_space_constraint(v, pltpu.HBM) for v in arrays]


def attend(place, x, wq, wk, wv, wg, gate_bias, wo, wl, wr):
    parts, residues, part_seqs, width = x.shape
    seqs = parts * part_seqs
    rows = residues * seqs
    operands = in_hbm(wq, wk, wv, wg, gate_bias.reshape(1, -1), wo, wl.T, wr.T)
    resident = pl.BlockSpec(memory_space=pltpu.VMEM)
    results = parts * (pltpu.HBM((part_seqs, residues * width), jnp.bfloat16),) + (
        jax.ShapeDtypeStruct((parts, 2, residues // 2, FACTOR_WIDTH, 2 * seqs), jnp.bfloat16),
    )
    macs = rows * width * (5 * width + 2 * FACTOR_WIDTH) + 2 * rows * ATTENTION_HEADS * width * seqs
    return pl.pallas_call(
        attend_kernel,
        out_shape=results,
        in_specs=[pl.BlockSpec(memory_space=pltpu.SMEM), resident]
        + [pl.BlockSpec(memory_space=pltpu.HBM)] * len(operands),
        out_specs=[pl.BlockSpec(memory_space=pltpu.HBM)] * parts + [resident],
        scratch_shapes=[
            pltpu.VMEM((rows, width), jnp.bfloat16),
            pltpu.VMEM((rows, width), jnp.bfloat16),
            pltpu.VMEM((rows, width), jnp.bfloat16),
            pltpu.VMEM((rows, width), jnp.float32),
            pltpu.VMEM((rows, width), jnp.bfloat16),
            pltpu.VMEM((5,) + wq.shape, jnp.bfloat16),
            pltpu.VMEM((1, width), jnp.float32),
            pltpu.VMEM((2, FACTOR_WIDTH, width), jnp.bfloat16),
            pltpu.VMEM((parts,) + results[0].shape, jnp.bfloat16),
            pltpu.VMEM((parts,) + results[0].shape, jnp.bfloat16),
            pltpu.SemaphoreType.DMA((len(operands) + parts,)),
        ],
        compiler_params=pltpu.CompilerParams(vmem_limit_bytes=32 * 1024 * 1024),
        cost_estimate=pl.CostEstimate(flops=2 * macs, bytes_accessed=4 * x.size * 2, transcendentals=rows * width),
        name="column_attention",
    )(place, x, *operands)


def first_of_four(at, cols):
    wide = MXU_SIDE // HALF * cols
    inside = jnp.where(at < wide, at, jnp.where(at < wide + HALF, at - HALF, at - wide - HALF))
    return inside // cols


def swapped(pair, wide):
    return [pair[:wide], pair[2 * wide - HALF:], pair[wide:2 * wide - HALF]]


def unswapped(pair, wide):
    return [pair[:wide], pair[wide + HALF:], pair[wide:wide + HALF]]


def right_kernel(
    factor_ref, w_ref, expand_ref, shrink_ref, rbd_ref, rbdt_ref, wec_ref, wt_ref, et_ref, st_ref, stage_s,
    *, seqs, cols, fold,
):
    each = factor_ref.shape[2]
    wide = fold * cols
    stage_lanes = stage_s.shape[1]
    low_half = lax.broadcasted_iota(jnp.int32, (1, LANES), 1) < HALF

    stage_s[:FACTOR_WIDTH * FACTOR_WIDTH, :LANES] = w_ref[...].astype(jnp.float32)
    for e in range(FACTOR_WIDTH):
        piece = stage_s[pl.ds(e, FACTOR_WIDTH, stride=FACTOR_WIDTH), :LANES]
        wec_ref[e * FACTOR_WIDTH:(e + 1) * FACTOR_WIDTH, :] = piece.astype(jnp.bfloat16)
    for b in range(FACTOR_WIDTH * FACTOR_WIDTH // LANES):
        block = wec_ref[b * LANES:(b + 1) * LANES, :].astype(jnp.float32)
        wt_ref[:, b * LANES:(b + 1) * LANES] = block.T.astype(jnp.bfloat16)
    et_ref[...] = expand_ref[...].astype(jnp.float32).T.astype(jnp.bfloat16)
    st_ref[...] = shrink_ref[...].astype(jnp.float32).T.astype(jnp.bfloat16)

    for p in range(cols // 2):
        block = factor_ref[p // each, 1, p % each].astype(jnp.float32)
        even = 2 * p * FACTOR_WIDTH
        odd = even + FACTOR_WIDTH
        if seqs % LANES == 0:
            stage_s[even:even + FACTOR_WIDTH, :] = block[:, :seqs]
            stage_s[odd:odd + FACTOR_WIDTH, :] = block[:, seqs:]
        else:
            stage_s[even:even + FACTOR_WIDTH, :] = block
            stage_s[odd:odd + FACTOR_WIDTH, :] = pltpu.roll(block, HALF, axis=1)

    row_k = first_of_four(lax.broadcasted_iota(jnp.int32, (2 * wide, 1), 0), cols)
    lane_k = first_of_four(lax.broadcasted_iota(jnp.int32, (1, 2 * wide), 1), cols)
    for e in range(0, FACTOR_WIDTH, 2):
        two = []
        for u in (e, e + 1):
            two += [stage_s[pl.ds(u, cols, stride=FACTOR_WIDTH), :]] * fold
        upright = jnp.concatenate(swapped(jnp.concatenate(two, axis=0), wide), axis=0)
        chunk, at = e // CHUNK, e % CHUNK * wide
        rolled = pltpu.roll(upright, HALF, axis=1) if seqs < LANES else None
        for v in range(fold * seqs // stage_lanes):
            if seqs < LANES:
                value = jnp.where(
                    low_half, jnp.where(row_k == 2 * v, upright, 0.0), jnp.where(row_k == 2 * v + 1, rolled, 0.0)
                )
            else:
                value = jnp.where(row_k == v, upright, 0.0)
            rbdt_ref[chunk, at:at + 2 * wide, v * stage_lanes:(v + 1) * stage_lanes] = value.astype(jnp.bfloat16)
        turned = upright.T[:seqs]
        for k in range(fold):
            value = jnp.where(lane_k == k, turned, 0.0).astype(jnp.bfloat16)
            rbd_ref[chunk, k * seqs:(k + 1) * seqs, at:at + 2 * wide] = value


def right_matrices(factors, outer_weight, expand_weight, shrink_weight):
    row_parts, _, each, _, lanes = factors.shape
    seqs, cols = lanes // 2, 2 * each * row_parts
    fold = MXU_SIDE // HALF
    channels, width = outer_weight.shape
    results = (
        jax.ShapeDtypeStruct((FACTOR_WIDTH // CHUNK, fold * seqs, CHUNK * fold * cols), jnp.bfloat16),
        jax.ShapeDtypeStruct((FACTOR_WIDTH // CHUNK, CHUNK * fold * cols, fold * seqs), jnp.bfloat16),
        jax.ShapeDtypeStruct((channels, width), jnp.bfloat16),
        jax.ShapeDtypeStruct((width, channels), jnp.bfloat16),
        jax.ShapeDtypeStruct(expand_weight.shape[::-1], jnp.bfloat16),
        jax.ShapeDtypeStruct(shrink_weight.shape[::-1], jnp.bfloat16),
    )
    resident = pl.BlockSpec(memory_space=pltpu.VMEM)
    return pl.pallas_call(
        functools.partial(right_kernel, seqs=seqs, cols=cols, fold=fold),
        out_shape=results,
        in_specs=[resident] * 4,
        out_specs=[resident] * len(results),
        scratch_shapes=[pltpu.VMEM((max(cols * FACTOR_WIDTH, channels), max(seqs, LANES)), jnp.float32)],
        compiler_params=pltpu.CompilerParams(vmem_limit_bytes=16 * 1024 * 1024),
        cost_estimate=pl.CostEstimate(flops=6 * 10**9, bytes_accessed=4 * results[0].size, transcendentals=0),
        name="right_matrices",
    )(factors, outer_weight, expand_weight, shrink_weight)


def pair_kernel(
    place_ref, *refs, seqs, cols, fold, unit, units, blocks,
):
    left_refs, refs = refs[:blocks], refs[blocks:]
    rbd_s, rbdt_s, wec_s, wt_s, et_ref, st_ref, pair_ref, cot_ref, back_ref = refs[:9]
    bias_ref, expand_ref, out_ref, gl_ref = refs[9:13]
    gr_refs, (outer_s, l_s, lt_s, stage_s, glacc_s, lblk_s, gr_s) = refs[13:-7], refs[-7:]
    step = pl.program_id(0)
    row_parts, each = left_refs[0].shape[:2]
    span = l_s.shape[0]
    groups = span // FACTOR_WIDTH
    wide = fold * cols
    scaling = 1.0 / seqs
    low_half = lax.broadcasted_iota(jnp.int32, (1, LANES), 1) < HALF

    @pl.when(step == 0)
    def _prologue():
        for n, ref in enumerate(left_refs):
            lblk_s[place_ref[n]] = ref[...]
        pairs = fold // 2
        for p in range(groups * pairs):
            column, inside = divmod(p, row_parts * each)
            block = lblk_s[column, inside // each, inside % each]
            g, at = p // pairs, p % pairs * 2 * seqs
            l_s[g * FACTOR_WIDTH:(g + 1) * FACTOR_WIDTH, at:at + 2 * seqs] = (
                block.astype(jnp.float32) * scaling
            ).astype(jnp.bfloat16)
        for b in range(span // LANES):
            block = l_s[b * LANES:(b + 1) * LANES, :].astype(jnp.float32)
            lt_s[:, b * LANES:(b + 1) * LANES] = block.T.astype(jnp.bfloat16)

        def some_outers(n, carry):
            outer_s[n] = dot_nn(l_s[...], rbd_s[n]).astype(jnp.bfloat16)
            return carry

        lax.fori_loop(0, outer_s.shape[0], some_outers, 0, unroll=2)

    def unit_rows(u):
        at = (step * units + u) * unit * FACTOR_WIDTH
        return pl.ds(pl.multiple_of(at, unit * FACTOR_WIDTH), unit * FACTOR_WIDTH)

    def group(block, g):
        return block[g * FACTOR_WIDTH:(g + 1) * FACTOR_WIDTH]

    def forward(u):
        stacked = []
        for e in range(0, FACTOR_WIDTH, 2):
            at = e % CHUNK * wide
            block = outer_s[e // CHUNK, unit_rows(u), at:at + 2 * wide]
            shared = block[:, LANES:2 * LANES]
            rolled = pltpu.roll(shared, HALF, axis=1)
            even, odd = [], []
            for g in range(0, unit, 2):
                a, b = block[:, :LANES], block[:, 2 * LANES:]
                even += [group(a, g), jnp.where(low_half, group(shared, g), group(rolled, g + 1)), group(a, g + 1)]
                odd += [group(b, g), jnp.where(low_half, group(rolled, g), group(shared, g + 1)), group(b, g + 1)]
            stacked += [jnp.concatenate(even, axis=1), jnp.concatenate(odd, axis=1)]
        projected = dot_nn(wt_s[...], jnp.concatenate(stacked, axis=0))
        middles, inverses, spreads = [], [], []
        for at in range(0, projected.shape[1], LANES):
            middle = pair_ref[step * units + u, :, at:at + LANES] + projected[:, at:at + LANES] + bias_ref[...]
            average = jnp.mean(middle, axis=0, keepdims=True)
            centred = middle - average
            variance = jnp.mean(centred * centred, axis=0, keepdims=True)
            inverse = lax.rsqrt(variance + EPSILON)
            middles.append(middle)
            inverses.append(inverse)
            spreads.append(centred * inverse)
        spread_low = jnp.concatenate([v.astype(jnp.bfloat16) for v in spreads], axis=1)
        return middles, inverses, spreads, dot_nn(et_ref[...], spread_low)

    def backward(u, middles, inverses, spreads, before):
        rows, pairs = before.shape
        hidden, back_before = [], []
        for at in range(0, rows, TILE):
            hidden_parts, back_parts = [], []
            for v in range(0, pairs, MXU_SIDE):
                x = before[at:at + TILE, v:v + MXU_SIDE]
                back = back_ref[step * units + u, at:at + TILE, v:v + MXU_SIDE].astype(jnp.float32)
                phi = 0.5 * (1.0 + lax.erf(x * 0.7071067811865476))
                slope = phi + x * jnp.exp(-0.5 * x * x) * 0.3989422804014327
                hidden_parts.append((x * phi).astype(jnp.bfloat16))
                back_parts.append((back * slope).astype(jnp.bfloat16))
            hidden.append(jnp.concatenate(hidden_parts, axis=1))
            back_before.append(jnp.concatenate(back_parts, axis=1))
        back_spread = dot_nn(expand_ref[...], jnp.concatenate(back_before, axis=0))
        change = dot_nn(st_ref[...], jnp.concatenate(hidden, axis=0))
        back_middle = []
        for n, at in enumerate(range(0, pairs, LANES)):
            back, spread = back_spread[:, at:at + LANES], spreads[n]
            centre_term = jnp.mean(back, axis=0, keepdims=True)
            slope_term = jnp.mean(back * spread, axis=0, keepdims=True)
            back = back - centre_term - spread * slope_term
            back = cot_ref[step * units + u, :, at:at + LANES] + inverses[n] * back
            back_middle.append(back.astype(jnp.bfloat16))
        result = (jnp.concatenate(middles, axis=1) + change).T
        pieces = []
        for g in range(0, unit, 2):
            pieces += unswapped(result[g * wide:(g + 2) * wide], wide)
        out_ref[u * unit * fold:(u + 1) * unit * fold] = jnp.concatenate(pieces, axis=0).reshape(
            unit * fold, cols, PAIR_W
        )
        back_outer = dot_nn(wec_s[...], jnp.concatenate(back_middle, axis=1)).astype(jnp.bfloat16)
        for e in range(0, FACTOR_WIDTH, 2):
            even, odd = group(back_outer, e), group(back_outer, e + 1)
            a, shared, b = [], [], []
            for g in range(0, unit, 2):
                at = g * wide
                of_even, of_odd = even[:, at + LANES:at + 2 * LANES], odd[:, at + LANES:at + 2 * LANES]
                a += [even[:, at:at + LANES], even[:, at + 2 * LANES:at + 3 * LANES]]
                b += [odd[:, at:at + LANES], odd[:, at + 2 * LANES:at + 3 * LANES]]
                shared += [
                    jnp.where(low_half, of_even, pltpu.roll(of_odd, HALF, axis=1)),
                    jnp.where(low_half, pltpu.roll(of_even, HALF, axis=1), of_odd),
                ]
            for n, pieces in enumerate((a, shared, b)):
                at = e % CHUNK * wide + n * LANES
                outer_s[e // CHUNK, unit_rows(u), at:at + LANES] = jnp.concatenate(pieces, axis=0)

    held = forward(0)
    for u in range(units):
        ahead = forward(u + 1) if u + 1 < units else None
        backward(u, *held)
        held = ahead

    @pl.when(step == pl.num_programs(0) - 1)
    def _epilogue():
        glacc_s[...] = jnp.zeros_like(glacc_s)
        empty = jnp.zeros((LANES - seqs % LANES, CHUNK * wide), jnp.float32) if seqs % LANES else None
        at = lax.broadcasted_iota(jnp.int32, (1, CHUNK * wide), 1)
        lane_k = first_of_four(lax.rem(at, 2 * wide), cols)

        def some(n, carry):
            back = outer_s[n]
            glacc_s[...] += dot_nn(back, rbdt_s[n])
            full = dot_nn(lt_s[...], back)
            compact = full[:seqs]
            for k in range(1, fold):
                compact = jnp.where(lane_k == k, full[k * seqs:(k + 1) * seqs], compact)
            if empty is not None:
                compact = jnp.concatenate([compact, empty], axis=0)
            turned = compact.T
            for p in range(CHUNK // 2):
                two = jnp.concatenate(unswapped(turned[2 * p * wide:2 * (p + 1) * wide], wide), axis=0)
                for u in range(2):
                    total = two[u * wide:u * wide + cols]
                    for k in range(1, fold):
                        total = total + two[u * wide + k * cols:u * wide + (k + 1) * cols]
                    stage_s[pl.ds(n * CHUNK + 2 * p + u, cols, stride=FACTOR_WIDTH), :] = total
            return carry

        lax.fori_loop(0, outer_s.shape[0], some, 0, unroll=2)
        for b in range(cols * FACTOR_WIDTH // LANES):
            block = stage_s[b * LANES:(b + 1) * LANES, :].T[:seqs].astype(jnp.bfloat16)
            gr_s[:, :, b * LANES:(b + 1) * LANES] = block.reshape(row_parts, -1, LANES)
        for k, ref in enumerate(gr_refs):
            ref[...] = gr_s[place_ref[blocks] ^ k]
        for b in range(span // LANES):
            block = glacc_s[b * LANES:(b + 1) * LANES, :].T * scaling
            for k in range(fold):
                at = k * span + b * LANES
                gl_ref[:, at:at + LANES] = block[k * seqs:(k + 1) * seqs].astype(jnp.bfloat16)


def turn_kernel(pair_ref, cot_ref, shrink_ref, after_ref, pair_out_ref, cot_out_ref, back_ref, *, wide):
    for source, target in ((pair_ref, pair_out_ref), (cot_ref, cot_out_ref)):
        rows = source[...].reshape(-1, PAIR_W)
        for at in range(0, rows.shape[0], 2 * wide):
            target[0, :, at:at + 2 * wide] = jnp.concatenate(swapped(rows[at:at + 2 * wide], wide), axis=0).T
    back_ref[0] = dot_nn(shrink_ref[...], cot_out_ref[0].astype(jnp.bfloat16)).astype(jnp.bfloat16)


def turned_pairs(pair_features, cotangent, shrink_weight, after):
    rows, cols, _ = pair_features.shape
    fold = MXU_SIDE // HALF
    count = rows // (UNIT * fold)
    pairs = UNIT * fold * cols
    hidden = shrink_weight.shape[0]
    results = (
        jax.ShapeDtypeStruct((count, PAIR_W, pairs), jnp.float32),
        jax.ShapeDtypeStruct((count, PAIR_W, pairs), jnp.float32),
        jax.ShapeDtypeStruct((count, hidden, pairs), jnp.bfloat16),
    )
    block = pl.BlockSpec((UNIT * fold, cols, PAIR_W), lambda n: (n, 0, 0))
    return pl.pallas_call(
        functools.partial(turn_kernel, wide=fold * cols),
        grid=(count,),
        out_shape=results,
        in_specs=[block, block, whole_block(shrink_weight.shape), pl.BlockSpec(memory_space=pl.ANY)],
        out_specs=[pl.BlockSpec((1,) + v.shape[1:], lambda n: (n, 0, 0)) for v in results],
        compiler_params=pltpu.CompilerParams(
            dimension_semantics=("arbitrary",), vmem_limit_bytes=24 * 1024 * 1024
        ),
        cost_estimate=pl.CostEstimate(
            flops=2 * 2 * count * pairs * hidden * PAIR_W, bytes_accessed=4 * 4 * pair_features.size, transcendentals=0
        ),
        name="turned_pairs",
    )(pair_features, cotangent, shrink_weight, after)


def pair_tile(place, lefts, matrices, turned, shape, outer_bias, expand_weight):
    seqs = lefts[0].shape[-1] // 2
    row_parts = lefts[0].shape[0]
    rows, cols, _ = shape
    fold = MXU_SIDE // HALF
    groups = rows // fold
    unit = UNIT
    units = 2 if groups % (2 * unit) == 0 else 1
    steps = groups // unit // units
    wide = fold * cols
    span = groups * FACTOR_WIDTH
    channels = FACTOR_WIDTH * FACTOR_WIDTH
    block = pl.BlockSpec((unit * units * fold, cols, PAIR_W), lambda n, place: (n, 0, 0))
    resident = pl.BlockSpec(memory_space=pltpu.VMEM)
    operands = (
        *lefts, *matrices, *turned, jnp.broadcast_to(outer_bias[:, None], (PAIR_W, LANES)), expand_weight,
    )
    results = (
        jax.ShapeDtypeStruct(shape, jnp.float32),
        jax.ShapeDtypeStruct((seqs, rows * FACTOR_WIDTH), jnp.bfloat16),
    ) + row_parts * (jax.ShapeDtypeStruct((seqs // row_parts, cols * FACTOR_WIDTH), jnp.bfloat16),)
    padded = groups * wide
    macs = 3 * FACTOR_WIDTH * span * fold * seqs * wide + padded * (2 * channels * MXU_SIDE + 8 * MXU_SIDE * MXU_SIDE)
    return pl.pallas_call(
        functools.partial(
            pair_kernel, seqs=seqs, cols=cols, fold=fold, unit=unit, units=units, blocks=len(lefts)
        ),
        grid_spec=pltpu.PrefetchScalarGridSpec(
            num_scalar_prefetch=1,
            grid=(steps,),
            in_specs=[resident] * len(operands),
            out_specs=[block] + [resident] * (len(results) - 1),
            scratch_shapes=[
                pltpu.VMEM((FACTOR_WIDTH // CHUNK, span, CHUNK * wide), jnp.bfloat16),
                pltpu.VMEM((span, fold * seqs), jnp.bfloat16),
                pltpu.VMEM((fold * seqs, span), jnp.bfloat16),
                pltpu.VMEM((cols * FACTOR_WIDTH, max(seqs, LANES)), jnp.float32),
                pltpu.VMEM((span, fold * seqs), jnp.float32),
                pltpu.VMEM((len(lefts),) + lefts[0].shape, jnp.bfloat16),
                pltpu.VMEM((row_parts,) + results[2].shape, jnp.bfloat16),
            ],
        ),
        out_shape=results,
        compiler_params=pltpu.CompilerParams(
            dimension_semantics=("arbitrary",), vmem_limit_bytes=36 * 1024 * 1024
        ),
        cost_estimate=pl.CostEstimate(
            flops=2 * macs, bytes_accessed=rows * cols * PAIR_W * 4, transcendentals=0
        ),
        name="pair_tile",
    )(place, *operands)


def finish_kernel(place_ref, *refs, residues, fold):
    *part_refs, gl_ref, updated_ref, left_ref, right_ref, x_s = refs
    upd_refs, gr_refs = part_refs[:len(part_refs) // 2], part_refs[len(part_refs) // 2:]
    part_seqs, res_count, width = updated_ref.shape
    total = gr_refs[0][...].astype(jnp.float32)
    for ref in gr_refs[1:]:
        total = total + ref[...].astype(jnp.float32)
    right_ref[...] = total
    for k, ref in enumerate(upd_refs):
        first = (place_ref[0] ^ k) * residues
        for r in range(residues):
            for n in range(width // LANES):
                at = r * width + n * LANES
                x_s[n, pl.ds(first + r, part_seqs, stride=res_count), :] = ref[:, at:at + LANES].astype(jnp.float32)
    for n in range(width // LANES):
        updated_ref[:, :, n * LANES:(n + 1) * LANES] = (
            x_s[n].reshape(part_seqs, res_count, LANES).astype(jnp.bfloat16)
        )
    total = gl_ref[0].astype(jnp.float32)
    for n in range(1, gl_ref.shape[0]):
        total = total + gl_ref[n].astype(jnp.float32)
    span = total.shape[1] // fold
    channel_block = lax.broadcasted_iota(jnp.int32, (1, LANES), 1) // FACTOR_WIDTH
    each = LANES // FACTOR_WIDTH
    for g in range(span // FACTOR_WIDTH):
        out = None
        for k in range(fold):
            at = k * span + g // each * LANES
            piece = total[:, at:at + LANES]
            shift = (k - g) % each * FACTOR_WIDTH
            piece = pltpu.roll(piece, shift, axis=1) if shift else piece
            out = piece if out is None else jnp.where(channel_block == k, piece, out)
        left_ref[:, g * LANES:(g + 1) * LANES] = out


def finish(place, returned, gr, gl, updated_shape):
    part_seqs, res_count, width = updated_shape
    residues = res_count // len(returned)
    results = (
        jax.ShapeDtypeStruct(updated_shape, jnp.bfloat16),
        jax.ShapeDtypeStruct(gl.shape[1:], jnp.float32),
        jax.ShapeDtypeStruct(gr[0].shape, jnp.float32),
    )
    resident = pl.BlockSpec(memory_space=pltpu.VMEM)
    return pl.pallas_call(
        functools.partial(finish_kernel, residues=residues, fold=MXU_SIDE // HALF),
        grid_spec=pltpu.PrefetchScalarGridSpec(
            num_scalar_prefetch=1,
            grid=(1,),
            in_specs=[resident] * (len(returned) + len(gr) + 1),
            out_specs=[whole_block(v.shape) for v in results],
            scratch_shapes=[pltpu.VMEM((width // LANES, part_seqs * res_count, LANES), jnp.float32)],
        ),
        out_shape=results,
        compiler_params=pltpu.CompilerParams(
            dimension_semantics=("arbitrary",), vmem_limit_bytes=16 * 1024 * 1024
        ),
        name="finish",
    )(place, *returned, *gr, gl)


def spread_out(q, count):
    return q if count % 2 else q % 2 * (count // 2) + q // 2


def local(
    alignment,
    pair_features,
    query_weight,
    key_weight,
    value_projection,
    gate_projection,
    gate_bias,
    output_projection,
    left_projection,
    right_projection,
    outer_weight,
    outer_bias,
    expand_weight,
    shrink_weight,
    cotangent,
):
    part_seqs, res_count, width = alignment.shape
    row_parts = lax.axis_size("row")
    col_parts = lax.axis_size("col")
    residues = res_count // row_parts
    own = jnp.transpose(alignment, (1, 0, 2)).reshape(row_parts, residues, part_seqs, width)
    columns = lax.all_to_all(own, "row", split_axis=0, concat_axis=0, tiled=True)
    row = lax.axis_index("row")
    own_row = row.astype(jnp.int32).reshape(1)
    *attended, factors = attend(
        own_row, columns, query_weight, key_weight, value_projection, gate_projection, gate_bias,
        output_projection, left_projection, right_projection,
    )

    factors = lax.all_to_all(factors, "row", split_axis=0, concat_axis=0, tiled=True)
    left = factors[:, 0]
    ratio = col_parts // row_parts
    lefts, place = [], []
    for m in range(ratio):
        moves = [
            (q * col_parts + ratio * r + b, r * col_parts + ratio * spread_out(q, row_parts) + (b + m) % ratio)
            for q in range(row_parts)
            for r in range(row_parts)
            for b in range(ratio)
        ]
        lefts.append(lax.ppermute(left, ("row", "col"), moves))
        place.append((lax.axis_index("col") + ratio - m) % ratio)
    matrices = right_matrices(factors, outer_weight, expand_weight, shrink_weight)
    turned = turned_pairs(pair_features, cotangent, shrink_weight, matrices[-1])

    def to_rows(values):
        return values[:1] + [
            lax.ppermute(v, "row", [(r, r ^ (k + 1)) for r in range(row_parts)]) for k, v in enumerate(values[1:])
        ]

    returned = to_rows(attended)
    lefts, returned = lax.optimization_barrier((lefts, returned))
    pair_out, gl, *gr = pair_tile(
        jnp.stack(place + [row]).astype(jnp.int32), lefts, matrices, turned, pair_features.shape, outer_bias,
        expand_weight,
    )
    seqs, gl_width = gl.shape
    gr = to_rows(gr)
    gl = lax.all_to_all(
        gl.reshape(col_parts, seqs // col_parts, gl_width), "col", split_axis=0, concat_axis=0, tiled=True
    )
    updated, grad_left, grad_right = finish(own_row, returned, gr, gl, alignment.shape)
    return (updated, pair_out, grad_left, grad_right)


def solution(mesh):
    return jax.shard_map(
        local,
        mesh=mesh,
        in_specs=(P("row", "col", None), P("row", "col", None)) + (P(),) * 12 + (P("row", "col", None),),
        out_specs=(P("row", "col", None), P("row", "col", None), P("col", "row"), P("row", "col")),
        check_vma=False,
    )
```

profile of v0, /device:TPU:0, one launch (start us, length us, event | category | flops | bytes accessed | tf_op | source)
XLA Modules:
  0.0 89.4 jit_solution(16623176115385347192)
XLA Ops:
  0.6 1.9 %copy.22 = bf16[48,16,256]{2,1,0:T(8,128)(2,1)} copy(bf16[48,16,256]{2,0,1:T(8,128)(2,1)} %bitcast.13) | data formatting | bytes 786432 | tf_op jit(solution)/shard_map/transpose | solution.py:579
  2.5 4.2 %all-to-all-start = ((bf16[4,12,16,256]{3,2,1,0:T(8,128)(2,1)}), bf16[4,12,16,256]{3,2,1,0:T(8,128)(2,1)S(1)}, u32[]{:S(2)}, u32[]{:S(2)}) async-start(bf16[4,12,16,256]{3,2,1,0:T(8,128)(2,1)} %bitcast.2), calls=%async_computation | async-start | bytes 786432 | tf_op jit(solution)/shard_map/all_to_all | solution.py:580
  6.7 0.0 copy-start.2
  6.7 0.0 copy-start.4
  6.7 0.0 copy-start.5
  6.7 7.4 %all-to-all-done.x_ref = bf16[4,12,16,256]{3,2,1,0:T(8,128)(2,1)S(1)} async-done(((bf16[4,12,16,256]{3,2,1,0:T(8,128)(2,1)}), bf16[4,12,16,256]{3,2,1,0:T(8,128)(2,1)S(1)}, u32[]{:S(2)}, u32[]{:S(2)}) %all-to-all-start) | async-done | bytes 393248 | tf_op jit(solution)/shard_map/all_to_all | solution.py:580
  14.2 7.3 %column_attention.1 = (bf16[16,3072]{1,0:T(8,128)(2,1)}, bf16[16,3072]{1,0:T(8,128)(2,1)}, bf16[16,3072]{1,0:T(8,128)(2,1)}, bf16[16,3072]{1,0:T(8,128)(2,1)}, bf16[4,2,6,32,128]{4,3,2,1,0:T(8,128)(2,1)}) custom-call(s32[1]{0:T(128)} %bitcast.place_ref, bf16[4,12,16,256]{3,2,1,0:T(8,128)(2,1)S(1)} %all-to-all-done.x_ref, bf16[256,256]{1,0:T(8,128)(2,1)} %wq_ref.1, ...), custom_call_target="tpu_custom_call" | custom-call | flops 931135488 | bytes 1572864 | tf_op jit(solution)/shard_map/column_attention/pallas_call | solution.py:122
  21.4 3.5 %all-to-all-start.1 = ((bf16[4,2,6,32,128]{4,3,2,1,0:T(8,128)(2,1)}), bf16[4,2,6,32,128]{4,3,2,1,0:T(8,128)(2,1)S(1)}, u32[]{:S(2)}, u32[]{:S(2)}) async-start(bf16[4,2,6,32,128]{4,3,2,1,0:T(8,128)(2,1)} %get-tuple-element.33), calls=%async_computation.1 | async-start | bytes 786432 | tf_op jit(solution)/shard_map/all_to_all | solution.py:588
  24.9 0.1 pad_add_fusion.place_ref
  25.0 0.5 collective-permute-start.2
  25.5 1.7 %collective-permute-start.3 = (bf16[16,3072]{1,0:T(8,128)(2,1)}, bf16[16,3072]{1,0:T(8,128)(2,1)S(1)}, u32[]{:S(2)}, u32[]{:S(2)}) collective-permute-start(bf16[16,3072]{1,0:T(8,128)(2,1)} %get-tuple-element.36), channel_id=1, source_target_pairs={{0,16},{8,24},{16,0},{24,8},{1,17},{9,25},{17,1},{25,9},{2,18},{10... | collective-permute-start | bytes 294920 | tf_op jit(solution)/shard_map/ppermute | solution.py:606
  27.1 0.0 collective-permute-start.4
  27.1 5.6 %all-to-all-done.1.factor_ref = bf16[4,2,6,32,128]{4,3,2,1,0:T(8,128)(2,1)S(1)} async-done(((bf16[4,2,6,32,128]{4,3,2,1,0:T(8,128)(2,1)}), bf16[4,2,6,32,128]{4,3,2,1,0:T(8,128)(2,1)S(1)}, u32[]{:S(2)}, u32[]{:S(2)}) %all-to-all-start.1) | async-done | bytes 393248 | tf_op jit(solution)/shard_map/all_to_all | solution.py:588
  32.8 0.0 copy-start
  32.8 0.0 copy-start.1
  32.8 2.2 %collective-permute-start.1 = (bf16[4,6,32,128]{3,2,1,0:T(8,128)(2,1)S(1)}, bf16[4,6,32,128]{3,2,1,0:T(8,128)(2,1)S(1)}, u32[]{:S(2)}, u32[]{:S(2)}) collective-permute-start(bf16[4,6,32,128]{3,2,1,0:T(8,128)(2,1)S(1)} %slice_bitcast_fusion), channel_id=1, source_target_pairs={{0,1},{1,0},{2,9},{3,8},{4,17},{5,16},{6,25},{7,24},{8,5},{9,4},{1... | collective-permute-start | bytes 589832 | tf_op jit(solution)/shard_map/ppermute | solution.py:599
  35.0 0.8 collective-permute-start
  35.9 0.0 copy-done.2
  35.9 0.0 copy-done.4
  35.9 0.0 copy-done.5
  35.9 2.9 %right_matrices.1 = (bf16[8,256,768]{2,1,0:T(8,128)(2,1)S(1)}, bf16[8,768,256]{2,1,0:T(8,128)(2,1)S(1)}, bf16[1024,128]{1,0:T(8,128)(2,1)S(1)}, bf16[128,1024]{1...) custom-call(bf16[4,2,6,32,128]{4,3,2,1,0:T(8,128)(2,1)S(1)} %all-to-all-done.1.factor_ref, ...), custom_call_target="tpu_custom_call" | custom-call | flops 6000000000 | bytes 6291456 | tf_op jit(solution)/shard_map/right_matrices/pallas_call | solution.py:228
  38.8 0.0 copy-done
  38.8 0.0 copy-done.1
  38.8 0.0 copy-start.6
  38.9 2.8 %turned_pairs.1 = (f32[6,128,768]{2,1,0:T(8,128)S(1)}, f32[6,128,768]{2,1,0:T(8,128)S(1)}, bf16[6,512,768]{2,1,0:T(8,128)(2,1)S(1)}) custom-call(f32[96,48,128]{2,1,0:T(8,128)S(1)} %copy-done, f32[96,48,128]{2,1,0:T(8,128)S(1)} %copy-done.1, bf16[512,128]{1,0:T(8,128)(2,1)S(1)} %copy-done.2, bf16[128,512]{1,0:T(8,128)(2,1)S(1)} %get-tuple-element.49.after_ref.refs_7_), custom_call_target="tpu_custom_call" | custom-call | flops 1207959552 | bytes 9437184 | tf_op jit(solution)/shard_map/turned_pairs/pallas_call | solution.py:424
  41.6 0.0 collective-permute-done.2.refs_1_
  41.6 0.0 collective-permute-done.3.refs_2_
  41.6 0.0 collective-permute-done.4.refs_3_
  41.7 2.7 %collective-permute-done.1.refs_1_ = bf16[4,6,32,128]{3,2,1,0:T(8,128)(2,1)S(1)} collective-permute-done((bf16[4,6,32,128]{3,2,1,0:T(8,128)(2,1)S(1)}, bf16[4,6,32,128]{3,2,1,0:T(8,128)(2,1)S(1)}, u32[]{:S(2)}, u32[]{:S(2)}) %collective-permute-start.1) | collective-permute-done | bytes 196640 | tf_op jit(solution)/shard_map/ppermute | solution.py:599
  44.3 0.0 collective-permute-done.refs_0_
  44.3 0.0 copy-done.6
  44.3 0.1 broadcast_in_dim.2.refs_11_
  44.4 0.0 copy-start.3
  44.4 23.3 %pair_tile.1 = (f32[96,48,128]{2,1,0:T(8,128)}, bf16[64,3072]{1,0:T(8,128)(2,1)}, bf16[16,1536]{1,0:T(8,128)(2,1)S(1)}, bf16[16,1536]{1,0:T(8,128)(2,1)S(1)}, bf...) custom-call(s32[3]{0:T(128)S(1)} %pad_add_fusion.place_ref, ...), custom_call_target="tpu_custom_call" | custom-call | flops 16911433728 | bytes 2359296 | tf_op jit(solution)/shard_map/pair_tile/pallas_call | solution.py:463
  67.7 8.1 %all-to-all-start.2 = ((bf16[8,8,3072]{2,1,0:T(8,128)(2,1)}), bf16[8,8,3072]{2,1,0:T(8,128)(2,1)S(1)}, u32[]{:S(2)}, u32[]{:S(2)}) async-start(bf16[8,8,3072]{2,1,0:T(8,128)(2,1)} %bitcast.9), calls=%async_computation.2 | async-start | bytes 786432 | tf_op jit(solution)/shard_map/all_to_all | solution.py:617
  75.8 0.4 collective-permute-start.5
  76.2 2.4 %collective-permute-start.6 = (bf16[16,1536]{1,0:T(8,128)(2,1)S(1)}, bf16[16,1536]{1,0:T(8,128)(2,1)S(1)}, u32[]{:S(2)}, u32[]{:S(2)}) collective-permute-start(bf16[16,1536]{1,0:T(8,128)(2,1)S(1)} %get-tuple-element.55), channel_id=1, source_target_pairs={{0,16},{8,24},{16,0},{24,8},{1,17},{9,25},{17,1},{25,9},{2,18},{10... | collective-permute-start | bytes 147464 | tf_op jit(solution)/shard_map/ppermute | solution.py:606
  78.6 0.1 collective-permute-start.7
  78.6 0.0 collective-permute-done.5.refs_5_
  78.6 2.3 %collective-permute-done.6.refs_6_ = bf16[16,1536]{1,0:T(8,128)(2,1)S(1)} collective-permute-done((bf16[16,1536]{1,0:T(8,128)(2,1)S(1)}, bf16[16,1536]{1,0:T(8,128)(2,1)S(1)}, u32[]{:S(2)}, u32[]{:S(2)}) %collective-permute-start.6) | collective-permute-done | bytes 49184 | tf_op jit(solution)/shard_map/ppermute | solution.py:606
  80.9 1.4 %collective-permute-done.7.refs_7_ = bf16[16,1536]{1,0:T(8,128)(2,1)S(1)} collective-permute-done((bf16[16,1536]{1,0:T(8,128)(2,1)S(1)}, bf16[16,1536]{1,0:T(8,128)(2,1)S(1)}, u32[]{:S(2)}, u32[]{:S(2)}) %collective-permute-start.7) | collective-permute-done | bytes 49184 | tf_op jit(solution)/shard_map/ppermute | solution.py:606
  82.3 5.9 %all-to-all-done.2.refs_8_ = bf16[8,8,3072]{2,1,0:T(8,128)(2,1)S(1)} async-done(((bf16[8,8,3072]{2,1,0:T(8,128)(2,1)}), bf16[8,8,3072]{2,1,0:T(8,128)(2,1)S(1)}, u32[]{:S(2)}, u32[]{:S(2)}) %all-to-all-start.2) | async-done | bytes 393248 | tf_op jit(solution)/shard_map/all_to_all | solution.py:617
  88.2 0.0 copy-done.3
  88.2 1.2 %finish.1 = (bf16[16,48,256]{2,1,0:T(8,128)(2,1)}, f32[8,3072]{1,0:T(8,128)}, f32[16,1536]{1,0:T(8,128)}) custom-call(s32[1]{0:T(128)} %bitcast.place_ref, bf16[16,3072]{1,0:T(8,128)(2,1)S(1)} %copy-done.3, bf16[16,3072]{1,0:T(8,128)(2,1)S(1)} %collective-permute-done.2.refs_1_, bf16[16,3072]{1,0:T(8,128)(2,1)S(1)} %collective-permute-done.3.refs_2_, ...), custom_call_target="tpu_custom_call" | custom-call | tf_op jit(solution)/shard_map/finish/pallas_call | solution.py:537
  (1 shorter events, 0.0 us)
Async XLA Ops:
  2.5 11.7 %all-to-all-start = ((bf16[4,12,16,256]{3,2,1,0:T(8,128)(2,1)}), bf16[4,12,16,256]{3,2,1,0:T(8,128)(2,1)S(1)}, u32[]{:S(2)}, u32[]{:S(2)}) async-start(bf16[4,12,16,256]{3,2,1,0:T(8,128)(2,1)} %bitcast.2), calls=%async_computation | async-start | bytes 786432 | tf_op jit(solution)/shard_map/all_to_all | solution.py:580
  6.7 29.1 %copy-start.2 = (bf16[512,128]{1,0:T(8,128)(2,1)S(1)}, bf16[512,128]{1,0:T(8,128)(2,1)}, u32[]{:S(2)}) copy-start(bf16[512,128]{1,0:T(8,128)(2,1)} %shrink_ref.3) | copy-start | bytes 393220
  6.7 29.2 %copy-start.4 = (bf16[1024,128]{1,0:T(8,128)(2,1)S(1)}, bf16[1024,128]{1,0:T(8,128)(2,1)}, u32[]{:S(2)}) copy-start(bf16[1024,128]{1,0:T(8,128)(2,1)} %w_ref.1) | copy-start | bytes 786436
  6.7 29.2 %copy-start.5 = (bf16[128,512]{1,0:T(8,128)(2,1)S(1)}, bf16[128,512]{1,0:T(8,128)(2,1)}, u32[]{:S(2)}) copy-start(bf16[128,512]{1,0:T(8,128)(2,1)} %refs_12_.1) | copy-start | bytes 393220
  21.4 11.4 %all-to-all-start.1 = ((bf16[4,2,6,32,128]{4,3,2,1,0:T(8,128)(2,1)}), bf16[4,2,6,32,128]{4,3,2,1,0:T(8,128)(2,1)S(1)}, u32[]{:S(2)}, u32[]{:S(2)}) async-start(bf16[4,2,6,32,128]{4,3,2,1,0:T(8,128)(2,1)} %get-tuple-element.33), calls=%async_computation.1 | async-start | bytes 786432 | tf_op jit(solution)/shard_map/all_to_all | solution.py:588
  25.0 16.6 %collective-permute-start.2 = (bf16[16,3072]{1,0:T(8,128)(2,1)}, bf16[16,3072]{1,0:T(8,128)(2,1)S(1)}, u32[]{:S(2)}, u32[]{:S(2)}) collective-permute-start(bf16[16,3072]{1,0:T(8,128)(2,1)} %get-tuple-element.35), channel_id=1, source_target_pairs={{0,8},{8,0},{16,24},{24,16},{1,9},{9,1},{17,25},{25,17},{2,10},{10... | collective-permute-start | bytes 294920 | tf_op jit(solution)/shard_map/ppermute | solution.py:606
  25.5 16.2 %collective-permute-start.3 = (bf16[16,3072]{1,0:T(8,128)(2,1)}, bf16[16,3072]{1,0:T(8,128)(2,1)S(1)}, u32[]{:S(2)}, u32[]{:S(2)}) collective-permute-start(bf16[16,3072]{1,0:T(8,128)(2,1)} %get-tuple-element.36), channel_id=1, source_target_pairs={{0,16},{8,24},{16,0},{24,8},{1,17},{9,25},{17,1},{25,9},{2,18},{10... | collective-permute-start | bytes 294920 | tf_op jit(solution)/shard_map/ppermute | solution.py:606
  27.1 14.5 %collective-permute-start.4 = (bf16[16,3072]{1,0:T(8,128)(2,1)}, bf16[16,3072]{1,0:T(8,128)(2,1)S(1)}, u32[]{:S(2)}, u32[]{:S(2)}) collective-permute-start(bf16[16,3072]{1,0:T(8,128)(2,1)} %get-tuple-element.37), channel_id=1, source_target_pairs={{0,24},{8,16},{16,8},{24,0},{1,25},{9,17},{17,9},{25,1},{2,26},{10... | collective-permute-start | bytes 294920 | tf_op jit(solution)/shard_map/ppermute | solution.py:606
  32.8 6.0 %copy-start = (f32[96,48,128]{2,1,0:T(8,128)S(1)}, f32[96,48,128]{2,1,0:T(8,128)}, u32[]{:S(2)}) copy-start(f32[96,48,128]{2,1,0:T(8,128)} %pair_ref.1) | copy-start | bytes 7077892
  32.8 6.0 %copy-start.1 = (f32[96,48,128]{2,1,0:T(8,128)S(1)}, f32[96,48,128]{2,1,0:T(8,128)}, u32[]{:S(2)}) copy-start(f32[96,48,128]{2,1,0:T(8,128)} %cot_ref.1) | copy-start | bytes 7077892
  32.8 11.5 %collective-permute-start.1 = (bf16[4,6,32,128]{3,2,1,0:T(8,128)(2,1)S(1)}, bf16[4,6,32,128]{3,2,1,0:T(8,128)(2,1)S(1)}, u32[]{:S(2)}, u32[]{:S(2)}) collective-permute-start(bf16[4,6,32,128]{3,2,1,0:T(8,128)(2,1)S(1)} %slice_bitcast_fusion), channel_id=1, source_target_pairs={{0,1},{1,0},{2,9},{3,8},{4,17},{5,16},{6,25},{7,24},{8,5},{9,4},{1... | collective-permute-start | bytes 589832 | tf_op jit(solution)/shard_map/ppermute | solution.py:599
  35.0 9.3 %collective-permute-start = (bf16[4,6,32,128]{3,2,1,0:T(8,128)(2,1)S(1)}, bf16[4,6,32,128]{3,2,1,0:T(8,128)(2,1)S(1)}, u32[]{:S(2)}, u32[]{:S(2)}) collective-permute-start(bf16[4,6,32,128]{3,2,1,0:T(8,128)(2,1)S(1)} %slice_bitcast_fusion), channel_id=1, source_target_pairs={{0,0},{1,1},{2,8},{3,9},{4,16},{5,17},{6,24},{7,25},{8,4},{9,5},{1... | collective-permute-start | bytes 589832 | tf_op jit(solution)/shard_map/ppermute | solution.py:599
  38.8 5.5 %copy-start.6 = (f32[128]{0:T(128)S(1)}, f32[128]{0:T(128)}, u32[]{:S(2)}) copy-start(f32[128]{0:T(128)} %param.26) | copy-start | bytes 1540
  44.4 43.8 %copy-start.3 = (bf16[16,3072]{1,0:T(8,128)(2,1)S(1)}, bf16[16,3072]{1,0:T(8,128)(2,1)}, u32[]{:S(2)}) copy-start(bf16[16,3072]{1,0:T(8,128)(2,1)} %get-tuple-element.38.refs_0_) | copy-start | bytes 294916
  67.7 20.5 %all-to-all-start.2 = ((bf16[8,8,3072]{2,1,0:T(8,128)(2,1)}), bf16[8,8,3072]{2,1,0:T(8,128)(2,1)S(1)}, u32[]{:S(2)}, u32[]{:S(2)}) async-start(bf16[8,8,3072]{2,1,0:T(8,128)(2,1)} %bitcast.9), calls=%async_computation.2 | async-start | bytes 786432 | tf_op jit(solution)/shard_map/all_to_all | solution.py:617
  75.8 2.9 %collective-permute-start.5 = (bf16[16,1536]{1,0:T(8,128)(2,1)S(1)}, bf16[16,1536]{1,0:T(8,128)(2,1)S(1)}, u32[]{:S(2)}, u32[]{:S(2)}) collective-permute-start(bf16[16,1536]{1,0:T(8,128)(2,1)S(1)} %get-tuple-element.54), channel_id=1, source_target_pairs={{0,8},{8,0},{16,24},{24,16},{1,9},{9,1},{17,25},{25,17},{2,10},{10... | collective-permute-start | bytes 147464 | tf_op jit(solution)/shard_map/ppermute | solution.py:606
  76.2 4.7 %collective-permute-start.6 = (bf16[16,1536]{1,0:T(8,128)(2,1)S(1)}, bf16[16,1536]{1,0:T(8,128)(2,1)S(1)}, u32[]{:S(2)}, u32[]{:S(2)}) collective-permute-start(bf16[16,1536]{1,0:T(8,128)(2,1)S(1)} %get-tuple-element.55), channel_id=1, source_target_pairs={{0,16},{8,24},{16,0},{24,8},{1,17},{9,25},{17,1},{25,9},{2,18},{10... | collective-permute-start | bytes 147464 | tf_op jit(solution)/shard_map/ppermute | solution.py:606
  78.6 3.7 %collective-permute-start.7 = (bf16[16,1536]{1,0:T(8,128)(2,1)S(1)}, bf16[16,1536]{1,0:T(8,128)(2,1)S(1)}, u32[]{:S(2)}, u32[]{:S(2)}) collective-permute-start(bf16[16,1536]{1,0:T(8,128)(2,1)S(1)} %get-tuple-element.56), channel_id=1, source_target_pairs={{0,24},{8,16},{16,8},{24,0},{1,25},{9,17},{17,9},{25,1},{2,26},{10... | collective-permute-start | bytes 147464 | tf_op jit(solution)/shard_map/ppermute | solution.py:606
where the time goes:
time: 89.8 us; the launch traced here: 89.4 us
  Pallas kernels  37.5 us (42%)
  waiting for transfers between devices  25.3 us (28%)
  starting transfers between devices  23.8 us (27%)
  local copies, waits for them, and re-layouts  1.98 us (2%)
    pallas_call x1, Pallas kernels, pair_tile(): pl.pallas_call(functools.partial(pair_kernel, seqs=seqs, cols=cols, fold=...  23.3 us
    all_to_all x1, starting transfers between devices, local(): lax.all_to_all(gl.reshape(col_parts, seqs // col_parts, gl_width), 'col',...  8.06 us
    all_to_all x1, waiting for transfers between devices, local(): lax.all_to_all(own, 'row', split_axis=0, concat_axis=0, tiled=True)  7.43 us
    pallas_call x1, Pallas kernels, attend(): pl.pallas_call(attend_kernel, out_shape=results, in_specs=[pl.BlockSpec(m...  7.25 us
    all_to_all x1, waiting for transfers between devices, local(): lax.all_to_all(gl.reshape(col_parts, seqs // col_parts, gl_width), 'col',...  5.92 us
    all_to_all x1, waiting for transfers between devices, local(): lax.all_to_all(factors, 'row', split_axis=0, concat_axis=0, tiled=True)  5.64 us
    ppermute x6, starting transfers between devices, to_rows(): lax.ppermute(v, 'row', [(r, r ^ k + 1) for r in range(row_parts)])  4.99 us
    all_to_all x1, starting transfers between devices, local(): lax.all_to_all(own, 'row', split_axis=0, concat_axis=0, tiled=True)  4.24 us
  transfers between devices with their start and end apart: 11, of which 6 were waited for; matrix products, arithmetic and copies ran while one was open for 0% of the time, Pallas kernels for 6%

commit v1 on v0

--- a/solution.py
+++ b/solution.py
@@ -38,8 +38,9 @@
 
 
 def attend_kernel(
-    place_ref, x_ref, wq_ref, wk_ref, wv_ref, wg_ref, bias_ref, wo_ref, wl_ref, wr_ref, *refs,
+    x_ref, wq_ref, wk_ref, wv_ref, wg_ref, bias_ref, wo_ref, wl_ref, wr_ref, *refs,
 ):
+    row = lax.axis_index("row")
     *upd_refs, factor_ref, q_s, k_s, v_s, g_s, a_s, w_s, bias_s, project_s, upd_s, ordered_s, sems = refs
     parts, residues, part_seqs, width = x_ref.shape
     seqs = parts * part_seqs
@@ -85,7 +86,7 @@
             upd_s[s, :, r * width:(r + 1) * width] = updated[begin:begin + part_seqs]
     leaving = []
     for k, ref in enumerate(upd_refs):
-        ordered_s[k] = upd_s[place_ref[0] ^ k]
+        ordered_s[k] = upd_s[row ^ k]
         leaving.append(pltpu.make_async_copy(ordered_s.at[k], ref, sems.at[len(sources) + k]))
         leaving[k].start()
     factor_norm = layer_normalise(updated).astype(jnp.bfloat16)
@@ -109,7 +110,7 @@
     return [pltpu.with_memory_space_constraint(v, pltpu.HBM) for v in arrays]
 
 
-def attend(place, x, wq, wk, wv, wg, gate_bias, wo, wl, wr):
+def attend(x, wq, wk, wv, wg, gate_bias, wo, wl, wr):
     parts, residues, part_seqs, width = x.shape
     seqs = parts * part_seqs
     rows = residues * seqs
@@ -122,8 +123,7 @@
     return pl.pallas_call(
         attend_kernel,
         out_shape=results,
-        in_specs=[pl.BlockSpec(memory_space=pltpu.SMEM), resident]
-        + [pl.BlockSpec(memory_space=pltpu.HBM)] * len(operands),
+        in_specs=[resident] + [pl.BlockSpec(memory_space=pltpu.HBM)] * len(operands),
         out_specs=[pl.BlockSpec(memory_space=pltpu.HBM)] * parts + [resident],
         scratch_shapes=[
             pltpu.VMEM((rows, width), jnp.bfloat16),
@@ -141,7 +141,7 @@
         compiler_params=pltpu.CompilerParams(vmem_limit_bytes=32 * 1024 * 1024),
         cost_estimate=pl.CostEstimate(flops=2 * macs, bytes_accessed=4 * x.size * 2, transcendentals=rows * width),
         name="column_attention",
-    )(place, x, *operands)
+    )(x, *operands)
 
 
 def first_of_four(at, cols):
@@ -578,10 +578,8 @@
     residues = res_count // row_parts
     own = jnp.transpose(alignment, (1, 0, 2)).reshape(row_parts, residues, part_seqs, width)
     columns = lax.all_to_all(own, "row", split_axis=0, concat_axis=0, tiled=True)
-    row = lax.axis_index("row")
-    own_row = row.astype(jnp.int32).reshape(1)
     *attended, factors = attend(
-        own_row, columns, query_weight, key_weight, value_projection, gate_projection, gate_bias,
+        columns, query_weight, key_weight, value_projection, gate_projection, gate_bias,
         output_projection, left_projection, right_projection,
     )
 
@@ -598,6 +596,8 @@
         ]
         lefts.append(lax.ppermute(left, ("row", "col"), moves))
         place.append((lax.axis_index("col") + ratio - m) % ratio)
+    row = lax.axis_index("row")
+    own_row = row.astype(jnp.int32).reshape(1)
     matrices = right_matrices(factors, outer_weight, expand_weight, shrink_weight)
     turned = turned_pairs(pair_features, cotangent, shrink_weight, matrices[-1])
 

time: 89.8 us -> 88.2 us (0.982)
  blocking collectives: 0 us -> 11.5 us
  waiting for transfers between devices: 25.3 us -> 18.8 us
  starting transfers between devices: 23.8 us -> 18 us
    all_to_all x0 -> x1, blocking collectives: none -> 11.5 us  [local(): lax.all_to_all(own, 'row', split_axis=0, concat_axis=0, tiled=True)]
    all_to_all x1 -> x0, waiting for transfers between devices: 7.43 us -> none  [local(): lax.all_to_all(own, 'row', split_axis=0, concat_axis=0, tiled=True)]
    all_to_all x1 -> x0, starting transfers between devices: 4.24 us -> none  [local(): lax.all_to_all(own, 'row', split_axis=0, concat_axis=0, tiled=True)]
    ppermute x2, waiting for transfers between devices: 2.67 us -> 3.63 us  [local(): lefts.append(lax.ppermute(left, ('row', 'col'), moves))]
    all_to_all x1, starting transfers between devices: 8.06 us -> 7.1 us  [local(): lax.all_to_all(gl.reshape(col_parts, seqs // col_parts, gl_width), 'col',...]
  transfers between devices with their start and end apart: 11 -> 10, of which waited for: 6 -> 5; matrix products, arithmetic and copies ran while one was open for 0% -> 0% of each run, Pallas kernels for 6% -> 6%
where the time goes in v1:
time: 88.2 us; the launch traced here: 87.8 us
  Pallas kernels  37.5 us (43%)
  waiting for transfers between devices  18.8 us (21%)
  starting transfers between devices  18 us (20%)
  blocking collectives  11.5 us (13%)
  local copies, waits for them, and re-layouts  1.24 us (1%)
    pallas_call x1, Pallas kernels, pair_tile(): pl.pallas_call(functools.partial(pair_kernel, seqs=seqs, cols=cols, fold=...  23.3 us
    all_to_all x1, blocking collectives, local(): lax.all_to_all(own, 'row', split_axis=0, concat_axis=0, tiled=True)  11.5 us
    pallas_call x1, Pallas kernels, attend(): pl.pallas_call(attend_kernel, out_shape=results, in_specs=[resident] + [p...  7.24 us
    all_to_all x1, starting transfers between devices, local(): lax.all_to_all(gl.reshape(col_parts, seqs // col_parts, gl_width), 'col',...  7.1 us
    all_to_all x1, waiting for transfers between devices, local(): lax.all_to_all(gl.reshape(col_parts, seqs // col_parts, gl_width), 'col',...  5.92 us
    all_to_all x1, waiting for transfers between devices, local(): lax.all_to_all(factors, 'row', split_axis=0, concat_axis=0, tiled=True)  5.64 us
    ppermute x6, starting transfers between devices, to_rows(): lax.ppermute(v, 'row', [(r, r ^ k + 1) for r in range(row_parts)])  4.99 us
    ppermute x6, waiting for transfers between devices, to_rows(): lax.ppermute(v, 'row', [(r, r ^ k + 1) for r in range(row_parts)])  3.63 us
  transfers between devices with their start and end apart: 10, of which 5 were waited for; matrix products, arithmetic and copies ran while one was open for 0% of the time, Pallas kernels for 6%

profile of v1, /device:TPU:0, one launch (start us, length us, event | category | flops | bytes accessed | tf_op | source)
XLA Modules:
  0.0 87.8 jit_solution(15441941202909475619)
XLA Ops:
  0.6 1.1 %copy.22 = bf16[48,16,256]{2,1,0:T(8,128)(2,1)S(1)} copy(bf16[48,16,256]{2,0,1:T(8,128)(2,1)} %bitcast.14) | data formatting | bytes 786432 | tf_op jit(solution)/shard_map/transpose | solution.py:579
  1.7 11.5 %all_to_all.15.x_ref = bf16[4,12,16,256]{3,2,1,0:T(8,128)(2,1)S(1)} all-to-all(bf16[4,12,16,256]{3,2,1,0:T(8,128)(2,1)S(1)} %bitcast.13), channel_id=1, replica_groups=mesh['row'=4,'col'=8] {'row'}, dimensions={0} | all-to-all | bytes 786432 | tf_op jit(solution)/shard_map/all_to_all | solution.py:580
  13.2 0.0 copy-start.2
  13.2 0.0 copy-start.4
  13.2 0.0 copy-start.5
  13.2 7.2 %column_attention.1 = (bf16[16,3072]{1,0:T(8,128)(2,1)}, bf16[16,3072]{1,0:T(8,128)(2,1)}, bf16[16,3072]{1,0:T(8,128)(2,1)}, bf16[16,3072]{1,0:T(8,128)(2,1)}, bf16[4,2,6,32,128]{4,3,2,1,0:T(8,128)(2,1)}) custom-call(bf16[4,12,16,256]{3,2,1,0:T(8,128)(2,1)S(1)} %all_to_all.15.x_ref, bf16[256,256]{1,0:T(8,128)(2,1)} %wq_ref.1, bf16[256,256]{1,0:T(8,128)(2,1)} %wk_ref.1, ...), custom_call_target="tpu_custom_call" | custom-call | flops 931135488 | bytes 1572864 | tf_op jit(solution)/shard_map/column_attention/pallas_call | solution.py:123
  20.5 3.5 %all-to-all-start.1 = ((bf16[4,2,6,32,128]{4,3,2,1,0:T(8,128)(2,1)}), bf16[4,2,6,32,128]{4,3,2,1,0:T(8,128)(2,1)S(1)}, u32[]{:S(2)}, u32[]{:S(2)}) async-start(bf16[4,2,6,32,128]{4,3,2,1,0:T(8,128)(2,1)} %get-tuple-element.33), calls=%async_computation.1 | async-start | bytes 786432 | tf_op jit(solution)/shard_map/all_to_all | solution.py:586
  24.0 0.1 pad_add_fusion.place_ref
  24.1 0.5 collective-permute-start.2
  24.5 1.7 %collective-permute-start.3 = (bf16[16,3072]{1,0:T(8,128)(2,1)}, bf16[16,3072]{1,0:T(8,128)(2,1)S(1)}, u32[]{:S(2)}, u32[]{:S(2)}) collective-permute-start(bf16[16,3072]{1,0:T(8,128)(2,1)} %get-tuple-element.36), channel_id=1, source_target_pairs={{0,16},{8,24},{16,0},{24,8},{1,17},{9,25},{17,1},{25,9},{2,18},{10... | collective-permute-start | bytes 294920 | tf_op jit(solution)/shard_map/ppermute | solution.py:606
  26.2 0.0 collective-permute-start.4
  26.2 5.6 %all-to-all-done.1.factor_ref = bf16[4,2,6,32,128]{4,3,2,1,0:T(8,128)(2,1)S(1)} async-done(((bf16[4,2,6,32,128]{4,3,2,1,0:T(8,128)(2,1)}), bf16[4,2,6,32,128]{4,3,2,1,0:T(8,128)(2,1)S(1)}, u32[]{:S(2)}, u32[]{:S(2)}) %all-to-all-start.1) | async-done | bytes 393248 | tf_op jit(solution)/shard_map/all_to_all | solution.py:586
  31.9 0.0 copy-start
  31.9 0.0 copy-start.1
  31.9 1.5 %collective-permute-start.1 = (bf16[4,6,32,128]{3,2,1,0:T(8,128)(2,1)S(1)}, bf16[4,6,32,128]{3,2,1,0:T(8,128)(2,1)S(1)}, u32[]{:S(2)}, u32[]{:S(2)}) collective-permute-start(bf16[4,6,32,128]{3,2,1,0:T(8,128)(2,1)S(1)} %slice_bitcast_fusion), channel_id=1, source_target_pairs={{0,1},{1,0},{2,9},{3,8},{4,17},{5,16},{6,25},{7,24},{8,5},{9,4},{1... | collective-permute-start | bytes 589832 | tf_op jit(solution)/shard_map/ppermute | solution.py:597
  33.4 0.8 collective-permute-start
  34.3 0.0 copy-done.2
  34.3 0.0 copy-done.4
  34.3 0.0 copy-done.5
  34.3 2.9 %right_matrices.1 = (bf16[8,256,768]{2,1,0:T(8,128)(2,1)S(1)}, bf16[8,768,256]{2,1,0:T(8,128)(2,1)S(1)}, bf16[1024,128]{1,0:T(8,128)(2,1)S(1)}, bf16[128,1024]{1...) custom-call(bf16[4,2,6,32,128]{4,3,2,1,0:T(8,128)(2,1)S(1)} %all-to-all-done.1.factor_ref, ...), custom_call_target="tpu_custom_call" | custom-call | flops 6000000000 | bytes 6291456 | tf_op jit(solution)/shard_map/right_matrices/pallas_call | solution.py:228
  37.2 0.0 copy-done
  37.2 0.0 copy-done.1
  37.3 0.0 copy-start.6
  37.3 2.8 %turned_pairs.1 = (f32[6,128,768]{2,1,0:T(8,128)S(1)}, f32[6,128,768]{2,1,0:T(8,128)S(1)}, bf16[6,512,768]{2,1,0:T(8,128)(2,1)S(1)}) custom-call(f32[96,48,128]{2,1,0:T(8,128)S(1)} %copy-done, f32[96,48,128]{2,1,0:T(8,128)S(1)} %copy-done.1, bf16[512,128]{1,0:T(8,128)(2,1)S(1)} %copy-done.2, bf16[128,512]{1,0:T(8,128)(2,1)S(1)} %get-tuple-element.49.after_ref.refs_7_), custom_call_target="tpu_custom_call" | custom-call | flops 1207959552 | bytes 9437184 | tf_op jit(solution)/shard_map/turned_pairs/pallas_call | solution.py:424
  40.0 0.0 collective-permute-done.2.refs_1_
  40.1 0.0 collective-permute-done.3.refs_2_
  40.1 0.0 collective-permute-done.4.refs_3_
  40.1 3.6 %collective-permute-done.1.refs_1_ = bf16[4,6,32,128]{3,2,1,0:T(8,128)(2,1)S(1)} collective-permute-done((bf16[4,6,32,128]{3,2,1,0:T(8,128)(2,1)S(1)}, bf16[4,6,32,128]{3,2,1,0:T(8,128)(2,1)S(1)}, u32[]{:S(2)}, u32[]{:S(2)}) %collective-permute-start.1) | collective-permute-done | bytes 196640 | tf_op jit(solution)/shard_map/ppermute | solution.py:597
  43.7 0.0 collective-permute-done.refs_0_
  43.7 0.0 copy-done.6
  43.7 0.1 broadcast_in_dim.2.refs_11_
  43.8 0.0 copy-start.3
  43.8 23.3 %pair_tile.1 = (f32[96,48,128]{2,1,0:T(8,128)}, bf16[64,3072]{1,0:T(8,128)(2,1)}, bf16[16,1536]{1,0:T(8,128)(2,1)S(1)}, bf16[16,1536]{1,0:T(8,128)(2,1)S(1)}, bf...) custom-call(s32[3]{0:T(128)S(1)} %pad_add_fusion.place_ref, ...), custom_call_target="tpu_custom_call" | custom-call | flops 16911433728 | bytes 2359296 | tf_op jit(solution)/shard_map/pair_tile/pallas_call | solution.py:463
  67.1 7.1 %all-to-all-start.2 = ((bf16[8,8,3072]{2,1,0:T(8,128)(2,1)}), bf16[8,8,3072]{2,1,0:T(8,128)(2,1)S(1)}, u32[]{:S(2)}, u32[]{:S(2)}) async-start(bf16[8,8,3072]{2,1,0:T(8,128)(2,1)} %bitcast.9), calls=%async_computation.2 | async-start | bytes 786432 | tf_op jit(solution)/shard_map/all_to_all | solution.py:617
  74.2 0.4 collective-permute-start.5
  74.6 2.4 %collective-permute-start.6 = (bf16[16,1536]{1,0:T(8,128)(2,1)S(1)}, bf16[16,1536]{1,0:T(8,128)(2,1)S(1)}, u32[]{:S(2)}, u32[]{:S(2)}) collective-permute-start(bf16[16,1536]{1,0:T(8,128)(2,1)S(1)} %get-tuple-element.55), channel_id=1, source_target_pairs={{0,16},{8,24},{16,0},{24,8},{1,17},{9,25},{17,1},{25,9},{2,18},{10... | collective-permute-start | bytes 147464 | tf_op jit(solution)/shard_map/ppermute | solution.py:606
  77.0 0.1 collective-permute-start.7
  77.1 0.0 collective-permute-done.5.refs_5_
  77.1 2.3 %collective-permute-done.6.refs_6_ = bf16[16,1536]{1,0:T(8,128)(2,1)S(1)} collective-permute-done((bf16[16,1536]{1,0:T(8,128)(2,1)S(1)}, bf16[16,1536]{1,0:T(8,128)(2,1)S(1)}, u32[]{:S(2)}, u32[]{:S(2)}) %collective-permute-start.6) | collective-permute-done | bytes 49184 | tf_op jit(solution)/shard_map/ppermute | solution.py:606
  79.3 1.4 %collective-permute-done.7.refs_7_ = bf16[16,1536]{1,0:T(8,128)(2,1)S(1)} collective-permute-done((bf16[16,1536]{1,0:T(8,128)(2,1)S(1)}, bf16[16,1536]{1,0:T(8,128)(2,1)S(1)}, u32[]{:S(2)}, u32[]{:S(2)}) %collective-permute-start.7) | collective-permute-done | bytes 49184 | tf_op jit(solution)/shard_map/ppermute | solution.py:606
  80.7 5.9 %all-to-all-done.2.refs_8_ = bf16[8,8,3072]{2,1,0:T(8,128)(2,1)S(1)} async-done(((bf16[8,8,3072]{2,1,0:T(8,128)(2,1)}), bf16[8,8,3072]{2,1,0:T(8,128)(2,1)S(1)}, u32[]{:S(2)}, u32[]{:S(2)}) %all-to-all-start.2) | async-done | bytes 393248 | tf_op jit(solution)/shard_map/all_to_all | solution.py:617
  86.6 0.0 copy-done.3
  86.6 1.2 %finish.1 = (bf16[16,48,256]{2,1,0:T(8,128)(2,1)}, f32[8,3072]{1,0:T(8,128)}, f32[16,1536]{1,0:T(8,128)}) custom-call(s32[1]{0:T(128)} %bitcast.place_ref, bf16[16,3072]{1,0:T(8,128)(2,1)S(1)} %copy-done.3, bf16[16,3072]{1,0:T(8,128)(2,1)S(1)} %collective-permute-done.2.refs_1_, bf16[16,3072]{1,0:T(8,128)(2,1)S(1)} %collective-permute-done.3.refs_2_, ...), custom_call_target="tpu_custom_call" | custom-call | tf_op jit(solution)/shard_map/finish/pallas_call | solution.py:537
  (1 shorter events, 0.0 us)
Async XLA Ops:
  13.2 21.1 %copy-start.2 = (bf16[512,128]{1,0:T(8,128)(2,1)S(1)}, bf16[512,128]{1,0:T(8,128)(2,1)}, u32[]{:S(2)}) copy-start(bf16[512,128]{1,0:T(8,128)(2,1)} %shrink_ref.3) | copy-start | bytes 393220
  13.2 21.1 %copy-start.4 = (bf16[1024,128]{1,0:T(8,128)(2,1)S(1)}, bf16[1024,128]{1,0:T(8,128)(2,1)}, u32[]{:S(2)}) copy-start(bf16[1024,128]{1,0:T(8,128)(2,1)} %w_ref.1) | copy-start | bytes 786436
  13.2 21.1 %copy-start.5 = (bf16[128,512]{1,0:T(8,128)(2,1)S(1)}, bf16[128,512]{1,0:T(8,128)(2,1)}, u32[]{:S(2)}) copy-start(bf16[128,512]{1,0:T(8,128)(2,1)} %refs_12_.1) | copy-start | bytes 393220
  20.5 11.4 %all-to-all-start.1 = ((bf16[4,2,6,32,128]{4,3,2,1,0:T(8,128)(2,1)}), bf16[4,2,6,32,128]{4,3,2,1,0:T(8,128)(2,1)S(1)}, u32[]{:S(2)}, u32[]{:S(2)}) async-start(bf16[4,2,6,32,128]{4,3,2,1,0:T(8,128)(2,1)} %get-tuple-element.33), calls=%async_computation.1 | async-start | bytes 786432 | tf_op jit(solution)/shard_map/all_to_all | solution.py:586
  24.1 16.0 %collective-permute-start.2 = (bf16[16,3072]{1,0:T(8,128)(2,1)}, bf16[16,3072]{1,0:T(8,128)(2,1)S(1)}, u32[]{:S(2)}, u32[]{:S(2)}) collective-permute-start(bf16[16,3072]{1,0:T(8,128)(2,1)} %get-tuple-element.35), channel_id=1, source_target_pairs={{0,8},{8,0},{16,24},{24,16},{1,9},{9,1},{17,25},{25,17},{2,10},{10... | collective-permute-start | bytes 294920 | tf_op jit(solution)/shard_map/ppermute | solution.py:606
  24.5 15.5 %collective-permute-start.3 = (bf16[16,3072]{1,0:T(8,128)(2,1)}, bf16[16,3072]{1,0:T(8,128)(2,1)S(1)}, u32[]{:S(2)}, u32[]{:S(2)}) collective-permute-start(bf16[16,3072]{1,0:T(8,128)(2,1)} %get-tuple-element.36), channel_id=1, source_target_pairs={{0,16},{8,24},{16,0},{24,8},{1,17},{9,25},{17,1},{25,9},{2,18},{10... | collective-permute-start | bytes 294920 | tf_op jit(solution)/shard_map/ppermute | solution.py:606
  26.2 13.9 %collective-permute-start.4 = (bf16[16,3072]{1,0:T(8,128)(2,1)}, bf16[16,3072]{1,0:T(8,128)(2,1)S(1)}, u32[]{:S(2)}, u32[]{:S(2)}) collective-permute-start(bf16[16,3072]{1,0:T(8,128)(2,1)} %get-tuple-element.37), channel_id=1, source_target_pairs={{0,24},{8,16},{16,8},{24,0},{1,25},{9,17},{17,9},{25,1},{2,26},{10... | collective-permute-start | bytes 294920 | tf_op jit(solution)/shard_map/ppermute | solution.py:606
  31.9 5.4 %copy-start = (f32[96,48,128]{2,1,0:T(8,128)S(1)}, f32[96,48,128]{2,1,0:T(8,128)}, u32[]{:S(2)}) copy-start(f32[96,48,128]{2,1,0:T(8,128)} %pair_ref.1) | copy-start | bytes 7077892
  31.9 5.4 %copy-start.1 = (f32[96,48,128]{2,1,0:T(8,128)S(1)}, f32[96,48,128]{2,1,0:T(8,128)}, u32[]{:S(2)}) copy-start(f32[96,48,128]{2,1,0:T(8,128)} %cot_ref.1) | copy-start | bytes 7077892
  31.9 11.8 %collective-permute-start.1 = (bf16[4,6,32,128]{3,2,1,0:T(8,128)(2,1)S(1)}, bf16[4,6,32,128]{3,2,1,0:T(8,128)(2,1)S(1)}, u32[]{:S(2)}, u32[]{:S(2)}) collective-permute-start(bf16[4,6,32,128]{3,2,1,0:T(8,128)(2,1)S(1)} %slice_bitcast_fusion), channel_id=1, source_target_pairs={{0,1},{1,0},{2,9},{3,8},{4,17},{5,16},{6,25},{7,24},{8,5},{9,4},{1... | collective-permute-start | bytes 589832 | tf_op jit(solution)/shard_map/ppermute | solution.py:597
  33.4 10.3 %collective-permute-start = (bf16[4,6,32,128]{3,2,1,0:T(8,128)(2,1)S(1)}, bf16[4,6,32,128]{3,2,1,0:T(8,128)(2,1)S(1)}, u32[]{:S(2)}, u32[]{:S(2)}) collective-permute-start(bf16[4,6,32,128]{3,2,1,0:T(8,128)(2,1)S(1)} %slice_bitcast_fusion), channel_id=1, source_target_pairs={{0,0},{1,1},{2,8},{3,9},{4,16},{5,17},{6,24},{7,25},{8,4},{9,5},{1... | collective-permute-start | bytes 589832 | tf_op jit(solution)/shard_map/ppermute | solution.py:597
  37.3 6.4 %copy-start.6 = (f32[128]{0:T(128)S(1)}, f32[128]{0:T(128)}, u32[]{:S(2)}) copy-start(f32[128]{0:T(128)} %param.26) | copy-start | bytes 1540
  43.8 42.8 %copy-start.3 = (bf16[16,3072]{1,0:T(8,128)(2,1)S(1)}, bf16[16,3072]{1,0:T(8,128)(2,1)}, u32[]{:S(2)}) copy-start(bf16[16,3072]{1,0:T(8,128)(2,1)} %get-tuple-element.38.refs_0_) | copy-start | bytes 294916
  67.1 19.5 %all-to-all-start.2 = ((bf16[8,8,3072]{2,1,0:T(8,128)(2,1)}), bf16[8,8,3072]{2,1,0:T(8,128)(2,1)S(1)}, u32[]{:S(2)}, u32[]{:S(2)}) async-start(bf16[8,8,3072]{2,1,0:T(8,128)(2,1)} %bitcast.9), calls=%async_computation.2 | async-start | bytes 786432 | tf_op jit(solution)/shard_map/all_to_all | solution.py:617
  74.2 2.9 %collective-permute-start.5 = (bf16[16,1536]{1,0:T(8,128)(2,1)S(1)}, bf16[16,1536]{1,0:T(8,128)(2,1)S(1)}, u32[]{:S(2)}, u32[]{:S(2)}) collective-permute-start(bf16[16,1536]{1,0:T(8,128)(2,1)S(1)} %get-tuple-element.54), channel_id=1, source_target_pairs={{0,8},{8,0},{16,24},{24,16},{1,9},{9,1},{17,25},{25,17},{2,10},{10... | collective-permute-start | bytes 147464 | tf_op jit(solution)/shard_map/ppermute | solution.py:606
  74.6 4.7 %collective-permute-start.6 = (bf16[16,1536]{1,0:T(8,128)(2,1)S(1)}, bf16[16,1536]{1,0:T(8,128)(2,1)S(1)}, u32[]{:S(2)}, u32[]{:S(2)}) collective-permute-start(bf16[16,1536]{1,0:T(8,128)(2,1)S(1)} %get-tuple-element.55), channel_id=1, source_target_pairs={{0,16},{8,24},{16,0},{24,8},{1,17},{9,25},{17,1},{25,9},{2,18},{10... | collective-permute-start | bytes 147464 | tf_op jit(solution)/shard_map/ppermute | solution.py:606
  77.0 3.7 %collective-permute-start.7 = (bf16[16,1536]{1,0:T(8,128)(2,1)S(1)}, bf16[16,1536]{1,0:T(8,128)(2,1)S(1)}, u32[]{:S(2)}, u32[]{:S(2)}) collective-permute-start(bf16[16,1536]{1,0:T(8,128)(2,1)S(1)} %get-tuple-element.56), channel_id=1, source_target_pairs={{0,24},{8,16},{16,8},{24,0},{1,25},{9,17},{17,9},{25,1},{2,26},{10... | collective-permute-start | bytes 147464 | tf_op jit(solution)/shard_map/ppermute | solution.py:606
